TPU v7x, 32 devices: a whole 2x2x4 slice. The times are simulated.
32 devices in a mesh: layer: 4 (over y, x), tile: 8 (over z, core).
Axes of the slice: x: 2, y: 2, z: 4, core: 2. Of those that a mesh axis runs over, the one named last changes fastest.
Arguments:
- blocks: bfloat16 [2560, 9, 128, 128], P(('layer', 'tile')), may hold values from -6 to 6
- prolong: bfloat16 [2560, 2048], P(('layer', 'tile')), may hold values from -0.5 to 0.5
- columns: int32 [2560, 9], P(('layer', 'tile')), may hold values from -1 to 143, as said below
- aggregate: int32 [2560], P(('layer', 'tile')), may hold values from 0 to 59, as said below
- coarse_slot: int32 [2560, 9], P(('layer', 'tile')), may hold values from 0 to 31
- send_rows: int32 [256, 8], P(('layer', 'tile')), may hold values from 0 to 79
Outputs:
- coarse: float32 [640, 8192], P(('layer', 'tile'))
Inputs may be any that keep to these rules, and one draw needn't show every extreme that they name: `columns`: slot 0 of every row is the row itself. A received code 80 + j * 8 + s appears in a device's rows if and only if the device has a neighbour in direction j (no wrap at the ends of the axes), and then every such code appears; -1 marks an absent block. `aggregate`: codes of a row i on its device are congruent to (i % 80) // 4 modulo 20. Codes of the second range never stand on the last tile, of the third never on the last layer.
All inputs are finite; a program needn't handle non-finite values.
Results may differ from a plain program's by a relative error of at most 0.0003.
Values may be sent and summed in bfloat16 or wider, within the bound.
A program may use at most 128 MiB of HBM per device.

v0:
```python
import jax
import jax.numpy as jnp
from jax import lax
from jax.sharding import PartitionSpec as P

CS = 32
AGG_DEV = 20


def with_halo(cells, sides, width):
    for axis, dim in sides:
        count = lax.axis_size(axis)
        ends = count - 1
        head = lax.slice_in_dim(cells, 0, width, axis=dim)
        tail = lax.slice_in_dim(cells, cells.shape[dim] - width, cells.shape[dim], axis=dim)
        cells = jnp.concatenate(
            [
                lax.ppermute(tail, axis, [(i, (i + 1) % count) for i in range(ends)]),
                cells,
                lax.ppermute(head, axis, [((i + 1) % count, i) for i in range(ends)]),
            ],
            axis=dim,
        )
    return cells


def shifted(value, axis, by):
    size = lax.axis_size(axis)
    pairs = [(i, i + by) for i in range(size) if 0 <= i + by < size]
    return lax.ppermute(value, axis, pairs)


def collect_rows(row_terms, codes, count):
    picker = (codes[:, None] == jnp.arange(count, dtype=jnp.int32)[None, :]).astype(jnp.float32)
    return jnp.dot(
        picker.T, row_terms, precision=lax.Precision.HIGHEST, preferred_element_type=jnp.float32
    )


def per_device(blocks, prolong, columns, aggregate, coarse_slot, send_rows):
    rows, links = columns.shape
    blk = blocks.shape[2]
    nnull = prolong.shape[1] // blk
    hcap = send_rows.shape[1]
    highest = lax.Precision.HIGHEST
    offsets = [
        (down, across) for down in (-1, 0, 1) for across in (-1, 0, 1) if down != 0 or across != 0
    ]
    outgoing = prolong[send_rows]
    pieces = []
    framed = with_halo(outgoing[None, None], (("layer", 0), ("tile", 1)), 1)
    for number, (down, across) in enumerate(offsets):
        pieces.append(framed[1 + down, 1 + across, 7 - number])
    ghost_rows = jnp.stack(pieces).reshape(8 * hcap, blk * nnull)
    table = jnp.concatenate([prolong, ghost_rows], axis=0)
    present = columns >= 0
    fetched = table[jnp.maximum(columns, 0)].reshape(rows, links, blk, nnull)
    product = jnp.einsum("rkab,rkbn->rkan", blocks, fetched, preferred_element_type=jnp.float32)
    own_basis = prolong.reshape(rows, blk, nnull).astype(jnp.float32)
    terms = jnp.einsum("ram,rkan->rkmn", own_basis, product, precision=highest)
    terms = jnp.where(present[:, :, None, None], terms, jnp.float32(0.0))
    slot_pick = (coarse_slot[:, :, None] == jnp.arange(CS, dtype=jnp.int32)[None, None, :]).astype(
        jnp.float32
    )
    row_terms = jnp.einsum("rks,rkmn->rsmn", slot_pick, terms, precision=highest).reshape(
        rows, CS * nnull * nnull
    )
    partial_value = collect_rows(row_terms, aggregate, 3 * AGG_DEV)
    owned = partial_value[:AGG_DEV]
    from_tile = shifted(partial_value[AGG_DEV : 2 * AGG_DEV], "tile", 1)
    from_layer = shifted(partial_value[2 * AGG_DEV :], "layer", 1)
    return owned + from_tile + from_layer


def solution(mesh):
    return jax.shard_map(
        per_device,
        mesh=mesh,
        in_specs=(
            P(("layer", "tile"), None, None, None),
            P(("layer", "tile"), None),
            P(("layer", "tile"), None),
            P(("layer", "tile")),
            P(("layer", "tile"), None),
            P(("layer", "tile"), None),
        ),
        out_specs=P(("layer", "tile"), None),
        check_vma=False,
    )
```

profile of v0, /device:TPU:13, one launch (start us, length us, event | category | flops | bytes accessed | tf_op | source)
XLA Modules:
  0.0 152.5 jit_solution(1351548657257499972)
XLA Ops:
  0.0 0.0 copy-start
  0.0 0.7 broadcast_maximum_fusion
  0.7 0.1 copy.11
  0.8 0.1 reshape.29
  1.0 0.7 compare_select_fusion
  1.7 0.1 reshape.21
  1.8 2.0 %gather_fusion = bf16[64,2048]{1,0:T(8,128)(2,1)S(1)} fusion(bf16[80,2048]{1,0:T(8,128)(2,1)} %param.7, s32[1024]{0:T(1024)S(1)} %get-tuple-element.8), kind=kCustom, calls=%fused_computation | custom fusion | bytes 524544 | tf_op jit(solution)/shard_map/gather | solution.py:49
  3.8 3.1 %collective-permute-start = (bf16[1,1,8,8,2048]{4,3,2,1,0:T(8,128)(2,1)S(1)}, bf16[1,1,8,8,2048]{4,3,2,1,0:T(8,128)(2,1)S(1)}, u32[]{:S(2)}, u32[]{:S(2)}) collective-permute-start(bf16[1,1,8,8,2048]{4,3,2,1,0:T(8,128)(2,1)S(1)} %bitcast.54), channel_id=1, source_target_pairs={{0,8},{8,16},{16,24},{1,9},{9,17},{17,25},{2,10},{10,18},{18,26},{... | collective-permute-start | bytes 786440 | tf_op jit(solution)/shard_map/ppermute | solution.py:18
  6.9 3.1 %collective-permute-start.1 = (bf16[1,1,8,8,2048]{4,3,2,1,0:T(8,128)(2,1)S(1)}, bf16[1,1,8,8,2048]{4,3,2,1,0:T(8,128)(2,1)S(1)}, u32[]{:S(2)}, u32[]{:S(2)}) collective-permute-start(bf16[1,1,8,8,2048]{4,3,2,1,0:T(8,128)(2,1)S(1)} %bitcast.55), channel_id=1, source_target_pairs={{8,0},{16,8},{24,16},{9,1},{17,9},{25,17},{10,2},{18,10},{26,18},{... | collective-permute-start | bytes 786440 | tf_op jit(solution)/shard_map/ppermute | solution.py:20
  10.0 3.8 %collective-permute-done = bf16[1,1,8,8,2048]{4,3,2,1,0:T(8,128)(2,1)S(1)} collective-permute-done((bf16[1,1,8,8,2048]{4,3,2,1,0:T(8,128)(2,1)S(1)}, bf16[1,1,8,8,2048]{4,3,2,1,0:T(8,128)(2,1)S(1)}, u32[]{:S(2)}, u32[]{:S(2)}) %collective-permute-start) | collective-permute-done | bytes 262176 | tf_op jit(solution)/shard_map/ppermute | solution.py:18
  13.8 3.7 %collective-permute-done.1 = bf16[1,1,8,8,2048]{4,3,2,1,0:T(8,128)(2,1)S(1)} collective-permute-done((bf16[1,1,8,8,2048]{4,3,2,1,0:T(8,128)(2,1)S(1)}, bf16[1,1,8,8,2048]{4,3,2,1,0:T(8,128)(2,1)S(1)}, u32[]{:S(2)}, u32[]{:S(2)}) %collective-permute-start.1) | collective-permute-done | bytes 262176 | tf_op jit(solution)/shard_map/ppermute | solution.py:20
  17.5 0.1 pad_maximum_fusion
  17.6 4.6 %collective-permute-start.2 = (bf16[3,1,8,8,2048]{4,3,2,1,0:T(8,128)(2,1)S(1)}, bf16[3,1,8,8,2048]{4,3,2,1,0:T(8,128)(2,1)S(1)}, u32[]{:S(2)}, u32[]{:S(2)}) collective-permute-start(bf16[3,1,8,8,2048]{4,3,2,1,0:T(8,128)(2,1)S(1)} %pad_maximum_fusion), channel_id=1, source_target_pairs={{0,1},{1,2},{2,3},{3,4},{4,5},{5,6},{6,7},{8,9},{9,10},{10,11},{11... | collective-permute-start | bytes 2359304 | tf_op jit(solution)/shard_map/ppermute | solution.py:18
  22.2 1.2 copy.12
  23.5 1.3 copy.14
  24.8 0.7 broadcast_compare_fusion
  25.5 0.1 copy.10
  25.6 1.4 copy.9
  27.1 1.9 %collective-permute-start.3 = (bf16[3,1,8,8,2048]{4,3,2,1,0:T(8,128)(2,1)S(1)}, bf16[3,1,8,8,2048]{4,3,2,1,0:T(8,128)(2,1)S(1)}, u32[]{:S(2)}, u32[]{:S(2)}) collective-permute-start(bf16[3,1,8,8,2048]{4,3,2,1,0:T(8,128)(2,1)S(1)} %pad_maximum_fusion), channel_id=1, source_target_pairs={{1,0},{2,1},{3,2},{4,3},{5,4},{6,5},{7,6},{9,8},{10,9},{11,10},{12... | collective-permute-start | bytes 2359304 | tf_op jit(solution)/shard_map/ppermute | solution.py:20
  29.0 2.2 %collective-permute-done.2 = bf16[3,1,8,8,2048]{4,3,2,1,0:T(8,128)(2,1)S(1)} collective-permute-done((bf16[3,1,8,8,2048]{4,3,2,1,0:T(8,128)(2,1)S(1)}, bf16[3,1,8,8,2048]{4,3,2,1,0:T(8,128)(2,1)S(1)}, u32[]{:S(2)}, u32[]{:S(2)}) %collective-permute-start.2) | collective-permute-done | bytes 786464 | tf_op jit(solution)/shard_map/ppermute | solution.py:18
  31.1 9.2 %collective-permute-done.3 = bf16[3,1,8,8,2048]{4,3,2,1,0:T(8,128)(2,1)S(1)} collective-permute-done((bf16[3,1,8,8,2048]{4,3,2,1,0:T(8,128)(2,1)S(1)}, bf16[3,1,8,8,2048]{4,3,2,1,0:T(8,128)(2,1)S(1)}, u32[]{:S(2)}, u32[]{:S(2)}) %collective-permute-start.3) | collective-permute-done | bytes 786464 | tf_op jit(solution)/shard_map/ppermute | solution.py:20
  40.4 0.0 copy-done
  40.5 3.4 %gather_fusion.1 = bf16[720,2048]{1,0:T(8,128)(2,1)S(1)} fusion(bf16[144,2048]{1,0:T(8,128)(2,1)S(1)} %pad_maximum_fusion.1, s32[1024]{0:T(1024)S(1)} %get-tuple-element.7), kind=kCustom, calls=%fused_computation.1 | custom fusion | bytes 5901120 | tf_op jit(solution)/shard_map/gather | solution.py:57
  43.9 20.5 %reshape.16 = bf16[80,9,128,16]{3,2,1,0:T(8,128)(2,1)} reshape(bf16[720,2048]{1,0:T(8,128)(2,1)S(1)} %gather_fusion.1) | data formatting | bytes 5898240 | tf_op jit(solution)/shard_map/reshape | solution.py:57
  64.4 0.0 copy-start.1
  64.4 18.8 %fusion.18 = f32[80,9,16,128]{3,2,1,0:T(8,128)S(1)} fusion(bf16[80,9,128,16]{3,2,1,0:T(8,128)(2,1)} %reshape.16, bf16[80,9,128,128]{3,2,1,0:T(8,128)(2,1)} %param.6), kind=kOutput, calls=%fused_computation.38 | convolution fusion | flops 377487360 | bytes 32440320 | tf_op jit(solution)/shard_map/rkab,rkbn->rkan/dot_general | solution.py:58
  83.2 0.0 copy-done.1
  83.2 4.5 %fusion = f32[80,9,16,16]{3,2,1,0:T(8,128)} fusion(bf16[80,128,16,1]{1,2,3,0:T(8,128)(2,1)S(1)} %copy-done.1, f32[80,9,16,128]{3,2,1,0:T(8,128)S(1)} %fusion.18), kind=kOutput, calls=%fused_computation.2 | convolution fusion | flops 283115520 | bytes 6963200 | tf_op jit(solution)/shard_map/ram,rkan->rkmn/dot_general | solution.py:60
  87.7 11.6 %copy.15 = f32[80,9,16,16]{1,2,3,0:T(8,128)} copy(f32[80,9,16,16]{3,2,1,0:T(8,128)} %fusion) | data formatting | bytes 1474560 | tf_op jit(solution)/shard_map/ram,rkan->rkmn/dot_general | solution.py:60
  99.2 0.0 copy-start.2
  99.3 5.5 %broadcast_select_fusion = f32[80,9,16,16]{1,2,3,0:T(8,128)S(1)} fusion(f32[80,9,16,16]{1,2,3,0:T(8,128)} %copy.15, pred[80,9]{1,0:T(8,128)(4,1)S(1)} %copy.10), kind=kLoop, calls=%fused_computation.4 | loop fusion | flops 184320 | bytes 1475280 | tf_op jit(solution)/shard_map/jit(_where)/select_n | solution.py:61
  104.7 0.0 copy-done.2
  104.7 7.8 %fusion.3 = f32[80,32,256]{1,2,0} fusion(f32[80,9,256]{1,2,0:T(8,128)S(1)} %bitcast.50, s32[80,9]{1,0:T(8,128)S(1)} %copy-done.2), kind=kOutput, calls=%fused_computation.9 | convolution fusion | flops 70801920 | bytes 3361600
  112.5 0.0 copy-start.3
  112.5 9.5 %copy.13 = f32[80,32,16,16]{0,3,2,1:T(8,128)} copy(f32[80,32,16,16]{1,3,2,0:T(8,128)} %bitcast.51) | data formatting | bytes 5242880 | tf_op jit(solution)/shard_map/rks,rkmn->rsmn/dot_general | solution.py:65
  122.0 0.0 copy-done.3
  122.0 4.9 %fusion.14 = f32[60,8192]{1,0:T(8,128)S(1)} fusion(f32[80,8192]{0,1:T(8,128)} %bitcast.52, s32[80]{0:T(128)S(1)} %copy-done.3), kind=kOutput, calls=%fused_computation.30 | convolution fusion | flops 471868800 | bytes 4587840 | tf_op jit(solution)/shard_map/dot_general | solution.py:35
  126.9 0.1 fusion.17
  127.0 1.9 %collective-permute-start.4 = (f32[20,8192]{1,0:T(8,128)S(1)}, f32[20,8192]{1,0:T(8,128)S(1)}, u32[]{:S(2)}, u32[]{:S(2)}) collective-permute-start(f32[20,8192]{1,0:T(8,128)S(1)} %get-tuple-element.5), channel_id=1, source_target_pairs={{0,1},{1,2},{2,3},{3,4},{4,5},{5,6},{6,7},{8,9},{9,10},{10,11},{11... | collective-permute-start | bytes 1966088 | tf_op jit(solution)/shard_map/ppermute | solution.py:30
  128.9 1.9 %collective-permute-start.5 = (f32[20,8192]{1,0:T(8,128)S(1)}, f32[20,8192]{1,0:T(8,128)S(1)}, u32[]{:S(2)}, u32[]{:S(2)}) collective-permute-start(f32[20,8192]{1,0:T(8,128)S(1)} %get-tuple-element.6), channel_id=1, source_target_pairs={{0,8},{8,16},{16,24},{1,9},{9,17},{17,25},{2,10},{10,18},{18,26},{... | collective-permute-start | bytes 1966088 | tf_op jit(solution)/shard_map/ppermute | solution.py:30
  130.9 7.0 %collective-permute-done.4 = f32[20,8192]{1,0:T(8,128)S(1)} collective-permute-done((f32[20,8192]{1,0:T(8,128)S(1)}, f32[20,8192]{1,0:T(8,128)S(1)}, u32[]{:S(2)}, u32[]{:S(2)}) %collective-permute-start.4) | collective-permute-done | bytes 655392 | tf_op jit(solution)/shard_map/ppermute | solution.py:30
  137.9 13.6 %collective-permute-done.5 = f32[20,8192]{1,0:T(8,128)S(1)} collective-permute-done((f32[20,8192]{1,0:T(8,128)S(1)}, f32[20,8192]{1,0:T(8,128)S(1)}, u32[]{:S(2)}, u32[]{:S(2)}) %collective-permute-start.5) | collective-permute-done | bytes 655392 | tf_op jit(solution)/shard_map/ppermute | solution.py:30
  151.4 1.1 fusion.2
  (10 shorter events, 0.1 us)
Async XLA Ops:
  0.0 40.4 %copy-start = (bf16[80,2048]{1,0:T(8,128)(2,1)S(1)}, bf16[80,2048]{1,0:T(8,128)(2,1)}, u32[]{:S(2)}) copy-start(bf16[80,2048]{1,0:T(8,128)(2,1)} %param.7) | copy-start | bytes 983044
  3.8 10.0 %collective-permute-start = (bf16[1,1,8,8,2048]{4,3,2,1,0:T(8,128)(2,1)S(1)}, bf16[1,1,8,8,2048]{4,3,2,1,0:T(8,128)(2,1)S(1)}, u32[]{:S(2)}, u32[]{:S(2)}) collective-permute-start(bf16[1,1,8,8,2048]{4,3,2,1,0:T(8,128)(2,1)S(1)} %bitcast.54), channel_id=1, source_target_pairs={{0,8},{8,16},{16,24},{1,9},{9,17},{17,25},{2,10},{10,18},{18,26},{... | collective-permute-start | bytes 786440 | tf_op jit(solution)/shard_map/ppermute | solution.py:18
  6.9 10.6 %collective-permute-start.1 = (bf16[1,1,8,8,2048]{4,3,2,1,0:T(8,128)(2,1)S(1)}, bf16[1,1,8,8,2048]{4,3,2,1,0:T(8,128)(2,1)S(1)}, u32[]{:S(2)}, u32[]{:S(2)}) collective-permute-start(bf16[1,1,8,8,2048]{4,3,2,1,0:T(8,128)(2,1)S(1)} %bitcast.55), channel_id=1, source_target_pairs={{8,0},{16,8},{24,16},{9,1},{17,9},{25,17},{10,2},{18,10},{26,18},{... | collective-permute-start | bytes 786440 | tf_op jit(solution)/shard_map/ppermute | solution.py:20
  17.6 13.6 %collective-permute-start.2 = (bf16[3,1,8,8,2048]{4,3,2,1,0:T(8,128)(2,1)S(1)}, bf16[3,1,8,8,2048]{4,3,2,1,0:T(8,128)(2,1)S(1)}, u32[]{:S(2)}, u32[]{:S(2)}) collective-permute-start(bf16[3,1,8,8,2048]{4,3,2,1,0:T(8,128)(2,1)S(1)} %pad_maximum_fusion), channel_id=1, source_target_pairs={{0,1},{1,2},{2,3},{3,4},{4,5},{5,6},{6,7},{8,9},{9,10},{10,11},{11... | collective-permute-start | bytes 2359304 | tf_op jit(solution)/shard_map/ppermute | solution.py:18
  27.1 13.3 %collective-permute-start.3 = (bf16[3,1,8,8,2048]{4,3,2,1,0:T(8,128)(2,1)S(1)}, bf16[3,1,8,8,2048]{4,3,2,1,0:T(8,128)(2,1)S(1)}, u32[]{:S(2)}, u32[]{:S(2)}) collective-permute-start(bf16[3,1,8,8,2048]{4,3,2,1,0:T(8,128)(2,1)S(1)} %pad_maximum_fusion), channel_id=1, source_target_pairs={{1,0},{2,1},{3,2},{4,3},{5,4},{6,5},{7,6},{9,8},{10,9},{11,10},{12... | collective-permute-start | bytes 2359304 | tf_op jit(solution)/shard_map/ppermute | solution.py:20
  64.4 18.8 %copy-start.1 = (bf16[80,128,16,1]{1,2,3,0:T(8,128)(2,1)S(1)}, bf16[80,128,16,1]{1,2,3,0:T(8,128)(2,1)}, u32[]{:S(2)}) copy-start(bf16[80,128,16,1]{1,2,3,0:T(8,128)(2,1)} %copy.14) | copy-start | bytes 983044
  99.2 5.5 %copy-start.2 = (s32[80,9]{1,0:T(8,128)S(1)}, s32[80,9]{1,0:T(8,128)}, u32[]{:S(2)}) copy-start(s32[80,9]{1,0:T(8,128)} %copy.9) | copy-start | bytes 8644
  112.5 9.5 %copy-start.3 = (s32[80]{0:T(128)S(1)}, s32[80]{0:T(128)}, u32[]{:S(2)}) copy-start(s32[80]{0:T(128)} %param.9) | copy-start | bytes 964
  127.0 10.8 %collective-permute-start.4 = (f32[20,8192]{1,0:T(8,128)S(1)}, f32[20,8192]{1,0:T(8,128)S(1)}, u32[]{:S(2)}, u32[]{:S(2)}) collective-permute-start(f32[20,8192]{1,0:T(8,128)S(1)} %get-tuple-element.5), channel_id=1, source_target_pairs={{0,1},{1,2},{2,3},{3,4},{4,5},{5,6},{6,7},{8,9},{9,10},{10,11},{11... | collective-permute-start | bytes 1966088 | tf_op jit(solution)/shard_map/ppermute | solution.py:30
  128.9 22.5 %collective-permute-start.5 = (f32[20,8192]{1,0:T(8,128)S(1)}, f32[20,8192]{1,0:T(8,128)S(1)}, u32[]{:S(2)}, u32[]{:S(2)}) collective-permute-start(f32[20,8192]{1,0:T(8,128)S(1)} %get-tuple-element.6), channel_id=1, source_target_pairs={{0,8},{8,16},{16,24},{1,9},{9,17},{17,25},{2,10},{10,18},{18,26},{... | collective-permute-start | bytes 1966088 | tf_op jit(solution)/shard_map/ppermute | solution.py:30
where the time goes:
time: 154 us; the launch traced here: 152 us
  local copies, waits for them, and re-layouts  51.6 us (34%)
  waiting for transfers between devices  39.4 us (26%)
  matrix products  35.9 us (23%)
  starting transfers between devices  16.6 us (11%)
  other arithmetic  8.81 us (6%)
    ppermute x2, waiting for transfers between devices, shifted(): return lax.ppermute(value, axis, pairs)  20.5 us
    reshape x1, local copies, waits for them, and re-layouts, per_device(): fetched = table[jnp.maximum(columns, 0)].reshape(rows, links, blk, nnull)  20.5 us
    dot_general x1, matrix products, per_device(): jnp.einsum('rkab,rkbn->rkan', blocks, fetched, preferred_element_type=jnp...  18.8 us
    ppermute x2, waiting for transfers between devices, with_halo(): lax.ppermute(head, axis, [((i + 1) % count, i) for i in range(ends)])  12.9 us
    dot_general x1, local copies, waits for them, and re-layouts, per_device(): terms = jnp.einsum('ram,rkan->rkmn', own_basis, product, precision=highest)  11.6 us
    dot_general x1, local copies, waits for them, and re-layouts, per_device(): jnp.einsum('rks,rkmn->rsmn', slot_pick, terms, precision=highest)  9.46 us
    unnamed x1, matrix products  7.78 us
    ppermute x2, starting transfers between devices, with_halo(): lax.ppermute(tail, axis, [(i, (i + 1) % count) for i in range(ends)])  7.76 us
  transfers between devices with their start and end apart: 6, of which 6 were waited for; matrix products, arithmetic and copies ran while one was open for 3% of the time, Pallas kernels for 0%

commit v1 on v0

v1 whole, which is shorter than its diff:
```python
import jax
import jax.numpy as jnp
from jax import lax
from jax.experimental import pallas as pl
from jax.experimental.pallas import tpu as pltpu
from jax.sharding import PartitionSpec as P

CS = 32
LANES = 128
MESH = pl.DeviceIdType.MESH
F32 = jnp.float32
BF16 = jnp.bfloat16


def iota(shape, dim):
    return lax.broadcasted_iota(jnp.int32, shape, dim)


def ones_where(cond):
    return jnp.where(cond, jnp.float32(1.0), jnp.float32(0.0))


def directions():
    return [(q // 3 - 1, q % 3 - 1) for q in range(9) if q != 4]


def block_transpose(x):
    i = iota((8, LANES), 0)
    j = iota((8, LANES), 1) // 16
    for d in (1, 2, 4):
        up = pltpu.roll(pltpu.roll(x, d, 0), LANES - 16 * d, 1)
        down = up if d == 4 else pltpu.roll(pltpu.roll(x, 8 - d, 0), 16 * d, 1)
        bi = (i // d) % 2
        bj = (j // d) % 2
        x = jnp.where(bi == bj, x, jnp.where(bi > bj, up, down))
    return x


def make_kernel(layers, tiles, rows, links, hcap, ga):
    aggs = rows // ga
    ghosts = 8 * hcap

    def kernel(
        columns, aggregate, slots, sends, x_ref, blocks,
        out,
        bbuf, table, stage, ghost, qbuf, own, to_tile, to_layer, from_tile, from_layer, lane_mask, slot_mask,
        b_sem, gs_sem, gr_sem, ts_sem, tr_sem, ls_sem, lr_sem,
    ):
        layer = lax.axis_index("layer")
        tile = lax.axis_index("tile")

        def load_blocks(g):
            return pltpu.make_async_copy(
                blocks.at[pl.ds(g * ga, ga)], bbuf.at[pl.ds(g * ga, ga)], b_sem.at[g]
            )

        @pl.loop(0, aggs)
        def _(g):
            load_blocks(g).start()

        dirs = []
        for dl, dt in directions():
            pl_, pt_ = layer + dl, tile + dt
            ok = (pl_ >= 0) & (pl_ < layers) & (pt_ >= 0) & (pt_ < tiles)
            dirs.append((ok, pl_, pt_))

        barrier = pltpu.get_barrier_semaphore()
        for ok, a, b in dirs:
            @pl.when(ok)
            def _():
                pl.semaphore_signal(barrier, inc=1, device_id=(a, b), device_id_type=MESH)

        for j in range(8):
            for s in range(hcap):
                stage[j, s * 16:(s + 1) * 16, :] = x_ref[sends[j, s]]

        peers = sum(jnp.where(ok, 1, 0) for ok, _, _ in dirs)
        pl.semaphore_wait(barrier, peers)

        def ghost_copy(j):
            ok, a, b = dirs[j]
            return pltpu.make_async_remote_copy(
                src_ref=stage.at[j],
                dst_ref=ghost.at[7 - j],
                send_sem=gs_sem.at[j],
                recv_sem=gr_sem.at[7 - j],
                device_id=(a, b),
                device_id_type=MESH,
            )

        for j in range(8):
            @pl.when(dirs[j][0])
            def _():
                ghost_copy(j).start()

        spread = ones_where(iota((128, 16), 0) // 8 == iota((128, 16), 1)).astype(BF16)
        keep = ones_where(iota((128, LANES), 1) // 16 == iota((128, LANES), 0) % 8)
        fold = ones_where(iota((LANES, LANES), 0) % 16 == iota((LANES, LANES), 1) % 16).astype(BF16)
        pick = ones_where(iota((16, LANES), 1) % 16 == iota((16, LANES), 0)).astype(BF16)
        for v in range(9):
            lane_mask[v] = ones_where(iota((16, LANES), 1) // 16 == v - 1).astype(BF16)
        for v in range(4):
            slot_mask[v] = ones_where(iota((64, LANES), 0) // 16 == v).astype(BF16)

        def expand(x):
            y = jnp.dot(spread, x, preferred_element_type=F32)
            return (y * keep).astype(BF16)

        @pl.loop(0, aggs)
        def _(g):
            load_blocks(g).wait()
            for r in range(ga):
                i = g * ga + r
                y = expand(x_ref[i])
                table[i] = jnp.dot(y, fold, preferred_element_type=F32).astype(BF16)
                turned = lax.dot_general(
                    pick, y, (((1,), (1,)), ((), ())), preferred_element_type=F32
                ).astype(BF16)
                row = jnp.concatenate([bbuf[i, k] for k in range(links)], axis=1)
                q = jnp.dot(turned, row, preferred_element_type=F32)
                hi = q.astype(BF16)
                qbuf[i, :16, :] = hi
                qbuf[i, 16:, :] = (q - hi.astype(F32)).astype(BF16)

        for j in range(8):
            ok = dirs[j][0]

            @pl.when(ok)
            def _():
                ghost_copy(j).wait_send()

            @pl.when(dirs[7 - j][0])
            def _():
                ghost_copy(j).wait_recv()

            @pl.when(jnp.logical_not(dirs[7 - j][0]))
            def _():
                ghost[7 - j] = jnp.zeros((hcap * 16, LANES), BF16)

        for j in range(8):
            @pl.loop(0, hcap // 4)
            def _(h):
                for r in range(4):
                    s = h * 4 + r
                    y = expand(ghost[j, pl.ds(pl.multiple_of(s * 16, 16), 16), :])
                    table[rows + j * hcap + s] = jnp.dot(
                        y, fold, preferred_element_type=F32
                    ).astype(BF16)

        def tile_copy(g):
            return pltpu.make_async_remote_copy(
                src_ref=to_tile.at[g],
                dst_ref=from_tile.at[g],
                send_sem=ts_sem.at[g],
                recv_sem=tr_sem.at[g],
                device_id=(layer, tile + 1),
                device_id_type=MESH,
            )

        def layer_copy(g):
            return pltpu.make_async_remote_copy(
                src_ref=to_layer.at[g],
                dst_ref=from_layer.at[g],
                send_sem=ls_sem.at[g],
                recv_sem=lr_sem.at[g],
                device_id=(layer + 1, tile),
                device_id_type=MESH,
            )

        has_next_tile = tile < tiles - 1
        has_next_layer = layer < layers - 1
        has_prev_tile = tile > 0
        has_prev_layer = layer > 0

        @pl.loop(0, aggs)
        def _(g):
            sums = [jnp.zeros((64, LANES), F32) for _ in range(3)]
            for r in range(ga):
                i = g * ga + r
                right = []
                left = []
                for k in range(links):
                    c = columns[i, k]
                    s = slots[i, k]
                    v = jnp.where(c >= 0, s % 8 + 1, 0)
                    right.append(table[jnp.maximum(c, 0)] * jnp.concatenate([lane_mask[v]] * 8, axis=0))
                    m = slot_mask[s // 8]
                    hi = qbuf[i, :16, k * 128:(k + 1) * 128]
                    lo = qbuf[i, 16:, k * 128:(k + 1) * 128]
                    left.append(
                        jnp.concatenate(
                            [jnp.concatenate([hi] * 4, axis=0) * m, jnp.concatenate([lo] * 4, axis=0) * m], axis=0
                        )
                    )
                both = jnp.dot(
                    jnp.concatenate(left, axis=1),
                    jnp.concatenate(right, axis=0),
                    preferred_element_type=F32,
                )
                term = both[:64] + both[64:]
                a = aggregate[i]
                sums[0] += term * jnp.where(a < aggs, jnp.float32(1), jnp.float32(0))
                sums[1] += term * jnp.where((a >= aggs) & (a < 2 * aggs), jnp.float32(1), jnp.float32(0))
                sums[2] += term * jnp.where(a >= 2 * aggs, jnp.float32(1), jnp.float32(0))
            own[g] = sums[0]
            to_tile[g] = sums[1]
            to_layer[g] = sums[2]

            @pl.when(has_next_layer)
            def _():
                layer_copy(g).start()

            @pl.when(has_next_tile)
            def _():
                tile_copy(g).start()

        @pl.when(jnp.logical_not(has_prev_tile))
        def _():
            from_tile[...] = jnp.zeros_like(from_tile)

        @pl.when(jnp.logical_not(has_prev_layer))
        def _():
            from_layer[...] = jnp.zeros_like(from_layer)

        @pl.loop(0, aggs)
        def _(g):
            @pl.when(has_prev_tile)
            def _():
                tile_copy(g).wait_recv()

            @pl.when(has_prev_layer)
            def _():
                layer_copy(g).wait_recv()

            for q in range(4):
                for h in range(2):
                    at = slice(q * 16 + h * 8, q * 16 + h * 8 + 8)
                    total = own[g, at, :] + from_tile[g, at, :] + from_layer[g, at, :]
                    out[g, pl.ds(q * 16 + h, 8, stride=2), :] = block_transpose(total)

        @pl.loop(0, aggs)
        def _(g):
            @pl.when(has_next_tile)
            def _():
                tile_copy(g).wait_send()

            @pl.when(has_next_layer)
            def _():
                layer_copy(g).wait_send()

    return kernel


def solution(mesh):
    layers = mesh.shape["layer"]
    tiles = mesh.shape["tile"]

    def per_device(blocks, prolong, columns, aggregate, coarse_slot, send_rows):
        rows, links = columns.shape
        blk = blocks.shape[2]
        nnull = prolong.shape[1] // blk
        hcap = send_rows.shape[1]
        ga = 4
        aggs = rows // ga
        x = prolong.reshape(rows, nnull, blk)
        smem = pl.BlockSpec(memory_space=pltpu.SMEM)
        vmem = pl.BlockSpec(memory_space=pltpu.VMEM)
        dma = pltpu.SemaphoreType.DMA
        part = pltpu.VMEM((aggs, 64, LANES), F32)
        flat = pl.pallas_call(
            make_kernel(layers, tiles, rows, links, hcap, ga),
            out_shape=jax.ShapeDtypeStruct((aggs, 64, LANES), F32),
            in_specs=[smem, smem, smem, smem, vmem, pl.BlockSpec(memory_space=pl.ANY)],
            out_specs=vmem,
            scratch_shapes=[
                pltpu.VMEM((rows, links, blk, blk), BF16),
                pltpu.VMEM((rows + 8 * hcap, blk, LANES), BF16),
                pltpu.VMEM((8, hcap * 16, LANES), BF16),
                pltpu.VMEM((8, hcap * 16, LANES), BF16),
                pltpu.VMEM((rows, 32, links * blk), BF16),
                part, part, part, part, part,
                pltpu.VMEM((9, 16, LANES), BF16),
                pltpu.VMEM((4, 64, LANES), BF16),
                dma((aggs,)), dma((8,)), dma((8,)),
                dma((aggs,)), dma((aggs,)), dma((aggs,)), dma((aggs,)),
            ],
            compiler_params=pltpu.CompilerParams(
                collective_id=0, has_side_effects=True, vmem_limit_bytes=56 * 1024 * 1024
            ),
            cost_estimate=pl.CostEstimate(
                flops=2 * rows * links * blk * blk * nnull, bytes_accessed=rows * links * blk * blk * 2, transcendentals=0
            ),
        )(columns, aggregate, coarse_slot, send_rows, x, blocks)
        return flat.reshape(aggs, 64 * LANES)

    return jax.shard_map(
        per_device,
        mesh=mesh,
        in_specs=(
            P(("layer", "tile"), None, None, None),
            P(("layer", "tile"), None),
            P(("layer", "tile"), None),
            P(("layer", "tile")),
            P(("layer", "tile"), None),
            P(("layer", "tile"), None),
        ),
        out_specs=P(("layer", "tile"), None),
        check_vma=False,
    )
```

time: 154 us -> 63.7 us (0.41)
  Pallas kernels: 0 us -> 55.7 us
  local copies, waits for them, and re-layouts: 51.6 us -> 7.06 us
  waiting for transfers between devices: 39.4 us -> 0 us
  matrix products: 35.9 us -> 0 us
  starting transfers between devices: 16.6 us -> 0 us
  other arithmetic: 8.81 us -> 0 us
    pallas_call x0 -> x1, Pallas kernels: none -> 55.7 us  [per_device(): pl.pallas_call(make_kernel(layers, tiles, rows, links, hcap, ga), out_sha...]
    ppermute x6 -> x0, waiting for transfers between devices: 39.4 us -> none  [the longest x2 20.5 us: shifted(): return lax.ppermute(value, axis, pairs)]
    dot_general x3 -> x0, matrix products: 28.2 us -> none  [the longest x1 18.8 us: per_device(): jnp.einsum('rkab,rkbn->rkan', blocks, fetched, preferred_element_type=jnp...]
    reshape x2 -> x0, local copies, waits for them, and re-layouts: 21.8 us -> none  [the longest x1 20.5 us: per_device(): fetched = table[jnp.maximum(columns, 0)].reshape(rows, links, blk, nnull)]
    dot_general x2 -> x0, local copies, waits for them, and re-layouts: 21 us -> none  [the longest x1 11.6 us: per_device(): terms = jnp.einsum('ram,rkan->rkmn', own_basis, product, precision=highest)]
    ppermute x6 -> x0, starting transfers between devices: 16.6 us -> none  [the longest x2 7.76 us: with_halo(): lax.ppermute(tail, axis, [(i, (i + 1) % count) for i in range(ends)])]
    unnamed x1 -> x0, matrix products: 7.78 us -> none
    select_n x2 -> x0, other arithmetic: 6.17 us -> none  [the longest x1 5.47 us: per_device(): terms = jnp.where(present[:, :, None, None], terms, jnp.float32(0.0))]
  transfers between devices with their start and end apart: 6 -> 0, of which waited for: 6 -> 0; matrix products, arithmetic and copies ran while one was open for 3% -> 0% of each run, Pallas kernels for 0% -> 0%
where the time goes in v1:
time: 63.7 us; the launch traced here: 62.7 us
  Pallas kernels  55.7 us (87%)
  local copies, waits for them, and re-layouts  7.06 us (11%)
    pallas_call x1, Pallas kernels, per_device(): pl.pallas_call(make_kernel(layers, tiles, rows, links, hcap, ga), out_sha...  55.7 us
    unnamed x5, local copies, waits for them, and re-layouts  7.06 us

profile of v1, /device:TPU:13, one launch (start us, length us, event | category | flops | bytes accessed | tf_op | source)
XLA Modules:
  0.0 62.7 jit_solution(17141279246907616665)
XLA Ops:
  0.0 1.4 %copy.7.columns = s32[80,9]{1,0:T(8,128)} copy(s32[80,9]{0,1:T(8,128)} %param.8) | data formatting | bytes 5760 | tf_op args[2]
  1.4 1.4 %copy.8.slots = s32[80,9]{1,0:T(8,128)} copy(s32[80,9]{0,1:T(8,128)} %param.10) | data formatting | bytes 5760 | tf_op args[4]
  2.8 1.8 %copy.9 = bf16[10,8,16,128]{3,2,1,0:T(8,128)(2,1)} copy(bf16[10,8,16,128]{3,1,2,0:T(8,128)(2,1)} %bitcast.7) | data formatting | bytes 655360
  4.6 55.7 %shard_map.64 = f32[20,64,128]{2,1,0:T(8,128)} custom-call(s32[80,9]{1,0:T(8,128)} %copy.7.columns, s32[80]{0:T(128)} %aggregate.1, s32[80,9]{1,0:T(8,128)} %copy.8.slots, s32[8,8]{1,0:T(8,128)} %sends.1, bf16[80,16,128]{2,1,0:T(8,128)(2,1)} %bitcast.6, bf16[80,9,128,128]{3,2,1,0:T(8,128)(2,1)} %blocks.1), custom_call_target="tpu_custom_call" | custom-call | flops 377487360 | bytes 23592960 | tf_op jit(solution)/shard_map/pallas_call | solution.py:270
  60.2 1.2 %pad = f32[24,64,128]{2,1,0:T(8,128)S(1)} pad(f32[20,64,128]{2,1,0:T(8,128)} %shard_map.64, f32[]{:T(128)} %constant.6), padding=0_4x0_0x0_0 | pad | bytes 1441796
  61.4 1.3 %copy.10 = f32[3,8,64,128]{3,1,2,0:T(8,128)} copy(f32[3,8,64,128]{3,2,1,0:T(8,128)S(1)} %bitcast.5) | data formatting | bytes 1572864

commit v2 on v1

--- a/solution.py
+++ b/solution.py
@@ -44,6 +44,7 @@
         columns, aggregate, slots, sends, x_ref, blocks,
         out,
         bbuf, table, stage, ghost, qbuf, own, to_tile, to_layer, from_tile, from_layer, lane_mask, slot_mask,
+        spread, spread_ghost, turned, final,
         b_sem, gs_sem, gr_sem, ts_sem, tr_sem, ls_sem, lr_sem,
     ):
         layer = lax.axis_index("layer")
@@ -70,9 +71,20 @@
             def _():
                 pl.semaphore_signal(barrier, inc=1, device_id=(a, b), device_id_type=MESH)
 
+        wanted = []
         for j in range(8):
+            row = jnp.zeros((hcap, rows), jnp.int32)
             for s in range(hcap):
-                stage[j, s * 16:(s + 1) * 16, :] = x_ref[sends[j, s]]
+                row = jnp.where(iota((hcap, rows), 0) == s, sends[j, s], row)
+            wanted.append(ones_where(row == iota((hcap, rows), 1)))
+        gathered = jnp.dot(
+            jnp.concatenate(wanted, axis=0).astype(BF16), x_ref[...], preferred_element_type=F32
+        )
+        for j in range(8):
+            part = gathered[j * hcap:(j + 1) * hcap]
+            stage[j] = jnp.concatenate(
+                [part[:, m * LANES:(m + 1) * LANES] for m in range(16)], axis=0
+            ).astype(BF16)
 
         peers = sum(jnp.where(ok, 1, 0) for ok, _, _ in dirs)
         pl.semaphore_wait(barrier, peers)
@@ -93,7 +105,14 @@
             def _():
                 ghost_copy(j).start()
 
-        spread = ones_where(iota((128, 16), 0) // 8 == iota((128, 16), 1)).astype(BF16)
+        for h in range(16):
+            spread[h * 128:(h + 1) * 128, :] = ones_where(
+                iota((128, 256), 1) == iota((128, 256), 0) // 8 * 16 + h
+            ).astype(BF16)
+        for h in range(hcap):
+            spread_ghost[h * 128:(h + 1) * 128, :] = ones_where(
+                iota((128, 16 * hcap), 1) == iota((128, 16 * hcap), 0) // 8 * hcap + h
+            ).astype(BF16)
         keep = ones_where(iota((128, LANES), 1) // 16 == iota((128, LANES), 0) % 8)
         fold = ones_where(iota((LANES, LANES), 0) % 16 == iota((LANES, LANES), 1) % 16).astype(BF16)
         pick = ones_where(iota((16, LANES), 1) % 16 == iota((16, LANES), 0)).astype(BF16)
@@ -102,22 +121,41 @@
         for v in range(4):
             slot_mask[v] = ones_where(iota((64, LANES), 0) // 16 == v).astype(BF16)
 
-        def expand(x):
-            y = jnp.dot(spread, x, preferred_element_type=F32)
-            return (y * keep).astype(BF16)
+        def expand(picker, x, count, at):
+            y = jnp.dot(picker, x, preferred_element_type=F32)
+            y = jnp.concatenate(
+                [(y[e * 128:(e + 1) * 128] * keep).astype(BF16) for e in range(count)], axis=0
+            )
+            t = jnp.dot(y, fold, preferred_element_type=F32).astype(BF16)
+            for e in range(count):
+                table[at + e] = t[e * 128:(e + 1) * 128]
+            return y
+
+        @pl.loop(0, rows // 16)
+        def _(h):
+            at = pl.multiple_of(h * 16, 16)
+            for half in range(2):
+                y = expand(
+                    spread[half * 1024:(half + 1) * 1024, :],
+                    jnp.concatenate(
+                        [x_ref[pl.ds(at, 16), m * LANES:(m + 1) * LANES] for m in range(16)], axis=0
+                    ),
+                    8,
+                    at + half * 8,
+                )
+                flipped = lax.dot_general(
+                    pick, y, (((1,), (1,)), ((), ())), preferred_element_type=F32
+                ).astype(BF16)
+                for e in range(8):
+                    turned[at + half * 8 + e] = flipped[:, e * 128:(e + 1) * 128]
 
         @pl.loop(0, aggs)
         def _(g):
             load_blocks(g).wait()
             for r in range(ga):
                 i = g * ga + r
-                y = expand(x_ref[i])
-                table[i] = jnp.dot(y, fold, preferred_element_type=F32).astype(BF16)
-                turned = lax.dot_general(
-                    pick, y, (((1,), (1,)), ((), ())), preferred_element_type=F32
-                ).astype(BF16)
                 row = jnp.concatenate([bbuf[i, k] for k in range(links)], axis=1)
-                q = jnp.dot(turned, row, preferred_element_type=F32)
+                q = jnp.dot(turned[i], row, preferred_element_type=F32)
                 hi = q.astype(BF16)
                 qbuf[i, :16, :] = hi
                 qbuf[i, 16:, :] = (q - hi.astype(F32)).astype(BF16)
@@ -137,15 +175,9 @@
             def _():
                 ghost[7 - j] = jnp.zeros((hcap * 16, LANES), BF16)
 
-        for j in range(8):
-            @pl.loop(0, hcap // 4)
-            def _(h):
-                for r in range(4):
-                    s = h * 4 + r
-                    y = expand(ghost[j, pl.ds(pl.multiple_of(s * 16, 16), 16), :])
-                    table[rows + j * hcap + s] = jnp.dot(
-                        y, fold, preferred_element_type=F32
-                    ).astype(BF16)
+        @pl.loop(0, 8)
+        def _(j):
+            expand(spread_ghost[...], ghost[j], hcap, rows + j * hcap)
 
         def tile_copy(g):
             return pltpu.make_async_remote_copy(
@@ -180,8 +212,8 @@
                 right = []
                 left = []
                 for k in range(links):
-                    c = columns[i, k]
-                    s = slots[i, k]
+                    c = columns[k, i]
+                    s = slots[k, i]
                     v = jnp.where(c >= 0, s % 8 + 1, 0)
                     right.append(table[jnp.maximum(c, 0)] * jnp.concatenate([lane_mask[v]] * 8, axis=0))
                     m = slot_mask[s // 8]
@@ -236,7 +268,7 @@
                 for h in range(2):
                     at = slice(q * 16 + h * 8, q * 16 + h * 8 + 8)
                     total = own[g, at, :] + from_tile[g, at, :] + from_layer[g, at, :]
-                    out[g, pl.ds(q * 16 + h, 8, stride=2), :] = block_transpose(total)
+                    final[pl.ds((q * 16 + h) * 24 + g, 8, stride=48), :] = block_transpose(total)
 
         @pl.loop(0, aggs)
         def _(g):
@@ -247,6 +279,9 @@
             @pl.when(has_next_layer)
             def _():
                 layer_copy(g).wait_send()
+
+        for m in range(64):
+            out[:, m * LANES:(m + 1) * LANES] = final[m * 24:m * 24 + aggs, :]
 
     return kernel
 
@@ -262,14 +297,13 @@
         hcap = send_rows.shape[1]
         ga = 4
         aggs = rows // ga
-        x = prolong.reshape(rows, nnull, blk)
         smem = pl.BlockSpec(memory_space=pltpu.SMEM)
         vmem = pl.BlockSpec(memory_space=pltpu.VMEM)
         dma = pltpu.SemaphoreType.DMA
         part = pltpu.VMEM((aggs, 64, LANES), F32)
-        flat = pl.pallas_call(
+        return pl.pallas_call(
             make_kernel(layers, tiles, rows, links, hcap, ga),
-            out_shape=jax.ShapeDtypeStruct((aggs, 64, LANES), F32),
+            out_shape=jax.ShapeDtypeStruct((aggs, 64 * LANES), F32),
             in_specs=[smem, smem, smem, smem, vmem, pl.BlockSpec(memory_space=pl.ANY)],
             out_specs=vmem,
             scratch_shapes=[
@@ -281,6 +315,10 @@
                 part, part, part, part, part,
                 pltpu.VMEM((9, 16, LANES), BF16),
                 pltpu.VMEM((4, 64, LANES), BF16),
+                pltpu.VMEM((2048, 256), BF16),
+                pltpu.VMEM((128 * hcap, 16 * hcap), BF16),
+                pltpu.VMEM((rows, 16, LANES), BF16),
+                pltpu.VMEM((64 * 24, LANES), F32),
                 dma((aggs,)), dma((8,)), dma((8,)),
                 dma((aggs,)), dma((aggs,)), dma((aggs,)), dma((aggs,)),
             ],
@@ -290,8 +328,7 @@
             cost_estimate=pl.CostEstimate(
                 flops=2 * rows * links * blk * blk * nnull, bytes_accessed=rows * links * blk * blk * 2, transcendentals=0
             ),
-        )(columns, aggregate, coarse_slot, send_rows, x, blocks)
-        return flat.reshape(aggs, 64 * LANES)
+        )(columns.T, aggregate, coarse_slot.T, send_rows, prolong, blocks)
 
     return jax.shard_map(
         per_device,

time: 63.7 us -> 41.3 us (0.65)
  the two profiles are of different devices: /device:TPU:13 before, /device:TPU:1 now
where the time goes in v2:
time: 41.3 us; the launch traced here: 41.2 us
  Pallas kernels  39.1 us (95%)
  local copies, waits for them, and re-layouts  2.06 us (5%)
    pallas_call x1, Pallas kernels, per_device(): pl.pallas_call(make_kernel(layers, tiles, rows, links, hcap, ga), out_sha...  39.1 us
    unnamed x1, local copies, waits for them, and re-layouts  2.06 us

profile of v2, /device:TPU:1, one launch (start us, length us, event | category | flops | bytes accessed | tf_op | source)
XLA Modules:
  0.0 41.2 jit_solution(9525946679206058882)
XLA Ops:
  0.0 39.1 %shard_map.64 = f32[20,8192]{1,0:T(8,128)} custom-call(s32[9,80]{1,0:T(8,128)} %bitcast.2, s32[80]{0:T(128)} %aggregate.1, s32[9,80]{1,0:T(8,128)} %bitcast.3, s32[8,8]{1,0:T(8,128)} %sends.1, bf16[80,2048]{1,0:T(8,128)(2,1)} %x_ref.1, bf16[80,9,128,128]{3,2,1,0:T(8,128)(2,1)} %blocks.1), custom_call_target="tpu_custom_call" | custom-call | flops 377487360 | bytes 23592960 | tf_op jit(solution)/shard_map/pallas_call | solution.py:304
  39.1 2.1 %copy.8 = f32[20,8192]{1,0:T(8,128)} copy(f32[20,8192]{1,0:T(8,128)} %shard_map.64) | data formatting | bytes 1310720

commit v3 on v2

--- a/solution.py
+++ b/solution.py
@@ -5,7 +5,8 @@
 from jax.experimental.pallas import tpu as pltpu
 from jax.sharding import PartitionSpec as P
 
-CS = 32
+LAG = 8
+PITCH = 129
 LANES = 128
 MESH = pl.DeviceIdType.MESH
 F32 = jnp.float32
@@ -44,7 +45,7 @@
         columns, aggregate, slots, sends, x_ref, blocks,
         out,
         bbuf, table, stage, ghost, qbuf, own, to_tile, to_layer, from_tile, from_layer, lane_mask, slot_mask,
-        spread, spread_ghost, turned, final,
+        wide, turned, final,
         b_sem, gs_sem, gr_sem, ts_sem, tr_sem, ls_sem, lr_sem,
     ):
         layer = lax.axis_index("layer")
@@ -105,44 +106,43 @@
             def _():
                 ghost_copy(j).start()
 
-        for h in range(16):
-            spread[h * 128:(h + 1) * 128, :] = ones_where(
-                iota((128, 256), 1) == iota((128, 256), 0) // 8 * 16 + h
-            ).astype(BF16)
-        for h in range(hcap):
-            spread_ghost[h * 128:(h + 1) * 128, :] = ones_where(
-                iota((128, 16 * hcap), 1) == iota((128, 16 * hcap), 0) // 8 * hcap + h
-            ).astype(BF16)
-        keep = ones_where(iota((128, LANES), 1) // 16 == iota((128, LANES), 0) % 8)
-        fold = ones_where(iota((LANES, LANES), 0) % 16 == iota((LANES, LANES), 1) % 16).astype(BF16)
-        pick = ones_where(iota((16, LANES), 1) % 16 == iota((16, LANES), 0)).astype(BF16)
+        place = jnp.concatenate(
+            [
+                ones_where(iota((LANES, LANES), 0) == iota((LANES, LANES), 1) % 16 + 16 * e).astype(BF16)
+                for e in range(8)
+            ],
+            axis=1,
+        )
+        pick = ones_where(iota((16, LANES), 1) == iota((16, LANES), 0)).astype(BF16)
         for v in range(9):
             lane_mask[v] = ones_where(iota((16, LANES), 1) // 16 == v - 1).astype(BF16)
         for v in range(4):
             slot_mask[v] = ones_where(iota((64, LANES), 0) // 16 == v).astype(BF16)
 
-        def expand(picker, x, count, at):
-            y = jnp.dot(picker, x, preferred_element_type=F32)
-            y = jnp.concatenate(
-                [(y[e * 128:(e + 1) * 128] * keep).astype(BF16) for e in range(count)], axis=0
-            )
-            t = jnp.dot(y, fold, preferred_element_type=F32).astype(BF16)
-            for e in range(count):
-                table[at + e] = t[e * 128:(e + 1) * 128]
-            return y
+        def expand(x, count, at):
+            for h in range(4):
+                y = jnp.dot(x, place[:, h * 256:(h + 1) * 256], preferred_element_type=F32)
+                for m in range(16):
+                    for c in range(0, count, 8):
+                        for e in range(2):
+                            wide[pl.ds(c * PITCH + 8 * m + 2 * h + e, 8, stride=PITCH), :] = y[
+                                m * count + c:m * count + c + 8, e * 128:(e + 1) * 128
+                            ]
+            for c in range(count):
+                table[at + c] = wide[c * PITCH:c * PITCH + 128, :].astype(BF16)
 
         @pl.loop(0, rows // 16)
         def _(h):
             at = pl.multiple_of(h * 16, 16)
+            expand(
+                jnp.concatenate(
+                    [x_ref[pl.ds(at, 16), m * LANES:(m + 1) * LANES] for m in range(16)], axis=0
+                ),
+                16,
+                at,
+            )
             for half in range(2):
-                y = expand(
-                    spread[half * 1024:(half + 1) * 1024, :],
-                    jnp.concatenate(
-                        [x_ref[pl.ds(at, 16), m * LANES:(m + 1) * LANES] for m in range(16)], axis=0
-                    ),
-                    8,
-                    at + half * 8,
-                )
+                y = jnp.concatenate([table[at + half * 8 + e] for e in range(8)], axis=0)
                 flipped = lax.dot_general(
                     pick, y, (((1,), (1,)), ((), ())), preferred_element_type=F32
                 ).astype(BF16)
@@ -177,7 +177,7 @@
 
         @pl.loop(0, 8)
         def _(j):
-            expand(spread_ghost[...], ghost[j], hcap, rows + j * hcap)
+            expand(ghost[j], hcap, rows + j * hcap)
 
         def tile_copy(g):
             return pltpu.make_async_remote_copy(
@@ -204,8 +204,15 @@
         has_prev_tile = tile > 0
         has_prev_layer = layer > 0
 
-        @pl.loop(0, aggs)
-        def _(g):
+        @pl.when(jnp.logical_not(has_prev_tile))
+        def _():
+            from_tile[...] = jnp.zeros_like(from_tile)
+
+        @pl.when(jnp.logical_not(has_prev_layer))
+        def _():
+            from_layer[...] = jnp.zeros_like(from_layer)
+
+        def combine(g):
             sums = [jnp.zeros((64, LANES), F32) for _ in range(3)]
             for r in range(ga):
                 i = g * ga + r
@@ -214,9 +221,9 @@
                 for k in range(links):
                     c = columns[k, i]
                     s = slots[k, i]
-                    v = jnp.where(c >= 0, s % 8 + 1, 0)
+                    v = jnp.where(c >= 0, (s & 7) + 1, 0)
                     right.append(table[jnp.maximum(c, 0)] * jnp.concatenate([lane_mask[v]] * 8, axis=0))
-                    m = slot_mask[s // 8]
+                    m = slot_mask[s >> 3]
                     hi = qbuf[i, :16, k * 128:(k + 1) * 128]
                     lo = qbuf[i, 16:, k * 128:(k + 1) * 128]
                     left.append(
@@ -238,6 +245,7 @@
             to_tile[g] = sums[1]
             to_layer[g] = sums[2]
 
+        def send(g):
             @pl.when(has_next_layer)
             def _():
                 layer_copy(g).start()
@@ -246,16 +254,7 @@
             def _():
                 tile_copy(g).start()
 
-        @pl.when(jnp.logical_not(has_prev_tile))
-        def _():
-            from_tile[...] = jnp.zeros_like(from_tile)
-
-        @pl.when(jnp.logical_not(has_prev_layer))
-        def _():
-            from_layer[...] = jnp.zeros_like(from_layer)
-
-        @pl.loop(0, aggs)
-        def _(g):
+        def receive(g):
             @pl.when(has_prev_tile)
             def _():
                 tile_copy(g).wait_recv()
@@ -264,11 +263,29 @@
             def _():
                 layer_copy(g).wait_recv()
 
+        def finish(g):
             for q in range(4):
                 for h in range(2):
                     at = slice(q * 16 + h * 8, q * 16 + h * 8 + 8)
                     total = own[g, at, :] + from_tile[g, at, :] + from_layer[g, at, :]
                     final[pl.ds((q * 16 + h) * 24 + g, 8, stride=48), :] = block_transpose(total)
+
+        @pl.loop(0, LAG)
+        def _(g):
+            combine(g)
+            send(g)
+
+        @pl.loop(LAG, aggs)
+        def _(g):
+            receive(g - LAG)
+            finish(g - LAG)
+            combine(g)
+            send(g)
+
+        @pl.loop(aggs - LAG, aggs)
+        def _(g):
+            receive(g)
+            finish(g)
 
         @pl.loop(0, aggs)
         def _(g):
@@ -315,8 +332,7 @@
                 part, part, part, part, part,
                 pltpu.VMEM((9, 16, LANES), BF16),
                 pltpu.VMEM((4, 64, LANES), BF16),
-                pltpu.VMEM((2048, 256), BF16),
-                pltpu.VMEM((128 * hcap, 16 * hcap), BF16),
+                pltpu.VMEM((16 * PITCH, LANES), F32),
                 pltpu.VMEM((rows, 16, LANES), BF16),
                 pltpu.VMEM((64 * 24, LANES), F32),
                 dma((aggs,)), dma((8,)), dma((8,)),

time: 41.3 us -> 35.6 us (0.86)
  the two profiles are of different devices: /device:TPU:1 before, /device:TPU:13 now
where the time goes in v3:
time: 35.6 us; the launch traced here: 35.5 us
  Pallas kernels  33.4 us (94%)
  local copies, waits for them, and re-layouts  2.06 us (6%)
    pallas_call x1, Pallas kernels, per_device(): pl.pallas_call(make_kernel(layers, tiles, rows, links, hcap, ga), out_sha...  33.4 us
    unnamed x1, local copies, waits for them, and re-layouts  2.06 us

profile of v3, /device:TPU:13, one launch (start us, length us, event | category | flops | bytes accessed | tf_op | source)
XLA Modules:
  0.0 35.5 jit_solution(2746819368462988989)
XLA Ops:
  0.0 33.4 %shard_map.64 = f32[20,8192]{1,0:T(8,128)} custom-call(s32[9,80]{1,0:T(8,128)} %bitcast.2, s32[80]{0:T(128)} %aggregate.1, s32[9,80]{1,0:T(8,128)} %bitcast.3, s32[8,8]{1,0:T(8,128)} %sends.1, bf16[80,2048]{1,0:T(8,128)(2,1)} %x_ref.1, bf16[80,9,128,128]{3,2,1,0:T(8,128)(2,1)} %blocks.1), custom_call_target="tpu_custom_call" | custom-call | flops 377487360 | bytes 23592960 | tf_op jit(solution)/shard_map/pallas_call | solution.py:321
  33.4 2.1 %copy.8 = f32[20,8192]{1,0:T(8,128)} copy(f32[20,8192]{1,0:T(8,128)} %shard_map.64) | data formatting | bytes 1310720

commit v4 on v3

--- a/solution.py
+++ b/solution.py
@@ -119,17 +119,17 @@
         for v in range(4):
             slot_mask[v] = ones_where(iota((64, LANES), 0) // 16 == v).astype(BF16)
 
-        def expand(x, count, at):
+        def expand(x, count, at, base=0):
             for h in range(4):
                 y = jnp.dot(x, place[:, h * 256:(h + 1) * 256], preferred_element_type=F32)
                 for m in range(16):
                     for c in range(0, count, 8):
                         for e in range(2):
-                            wide[pl.ds(c * PITCH + 8 * m + 2 * h + e, 8, stride=PITCH), :] = y[
+                            wide[pl.ds(base + c * PITCH + 8 * m + 2 * h + e, 8, stride=PITCH), :] = y[
                                 m * count + c:m * count + c + 8, e * 128:(e + 1) * 128
                             ]
             for c in range(count):
-                table[at + c] = wide[c * PITCH:c * PITCH + 128, :].astype(BF16)
+                table[at + c] = wide[base + c * PITCH:base + c * PITCH + 128, :].astype(BF16)
 
         @pl.loop(0, rows // 16)
         def _(h):
@@ -175,9 +175,10 @@
             def _():
                 ghost[7 - j] = jnp.zeros((hcap * 16, LANES), BF16)
 
-        @pl.loop(0, 8)
+        @pl.loop(0, 4)
         def _(j):
-            expand(ghost[j], hcap, rows + j * hcap)
+            for e in range(2):
+                expand(ghost[2 * j + e], hcap, rows + (2 * j + e) * hcap, e * 8 * PITCH)
 
         def tile_copy(g):
             return pltpu.make_async_remote_copy(
@@ -268,7 +269,7 @@
                 for h in range(2):
                     at = slice(q * 16 + h * 8, q * 16 + h * 8 + 8)
                     total = own[g, at, :] + from_tile[g, at, :] + from_layer[g, at, :]
-                    final[pl.ds((q * 16 + h) * 24 + g, 8, stride=48), :] = block_transpose(total)
+                    final[pl.ds((q * 16 + h) * 25 + g, 8, stride=50), :] = block_transpose(total)
 
         @pl.loop(0, LAG)
         def _(g):
@@ -298,7 +299,7 @@
                 layer_copy(g).wait_send()
 
         for m in range(64):
-            out[:, m * LANES:(m + 1) * LANES] = final[m * 24:m * 24 + aggs, :]
+            out[:, m * LANES:(m + 1) * LANES] = final[m * 25:m * 25 + aggs, :]
 
     return kernel
 
@@ -334,7 +335,7 @@
                 pltpu.VMEM((4, 64, LANES), BF16),
                 pltpu.VMEM((16 * PITCH, LANES), F32),
                 pltpu.VMEM((rows, 16, LANES), BF16),
-                pltpu.VMEM((64 * 24, LANES), F32),
+                pltpu.VMEM((64 * 25, LANES), F32),
                 dma((aggs,)), dma((8,)), dma((8,)),
                 dma((aggs,)), dma((aggs,)), dma((aggs,)), dma((aggs,)),
             ],

time: 35.6 us -> 35 us (0.983)
  Pallas kernels: 33.4 us -> 32.7 us
    pallas_call x1, Pallas kernels: 33.4 us -> 32.7 us  [per_device(): pl.pallas_call(make_kernel(layers, tiles, rows, links, hcap, ga), out_sha...]
where the time goes in v4:
time: 35 us; the launch traced here: 34.8 us
  Pallas kernels  32.7 us (93%)
  local copies, waits for them, and re-layouts  2.06 us (6%)
    pallas_call x1, Pallas kernels, per_device(): pl.pallas_call(make_kernel(layers, tiles, rows, links, hcap, ga), out_sha...  32.7 us
    unnamed x1, local copies, waits for them, and re-layouts  2.06 us

profile of v4, /device:TPU:13, one launch (start us, length us, event | category | flops | bytes accessed | tf_op | source)
XLA Modules:
  0.0 34.8 jit_solution(918220093770861505)
XLA Ops:
  0.0 32.7 %shard_map.64 = f32[20,8192]{1,0:T(8,128)} custom-call(s32[9,80]{1,0:T(8,128)} %bitcast.2, s32[80]{0:T(128)} %aggregate.1, s32[9,80]{1,0:T(8,128)} %bitcast.3, s32[8,8]{1,0:T(8,128)} %sends.1, bf16[80,2048]{1,0:T(8,128)(2,1)} %x_ref.1, bf16[80,9,128,128]{3,2,1,0:T(8,128)(2,1)} %blocks.1), custom_call_target="tpu_custom_call" | custom-call | flops 377487360 | bytes 23592960 | tf_op jit(solution)/shard_map/pallas_call | solution.py:322
  32.7 2.1 %copy.8 = f32[20,8192]{1,0:T(8,128)} copy(f32[20,8192]{1,0:T(8,128)} %shard_map.64) | data formatting | bytes 1310720
